TPU v7x, 256 devices: a whole 4x4x8 slice. The times are simulated.
256 devices in a mesh: dp: 32 (over z, x), mp: 8 (over y, core).
Axes of the slice: x: 4, y: 4, z: 8, core: 2. Of those that a mesh axis runs over, the one named last changes fastest.
Arguments:
- grads: bfloat16 [32, 256, 28672], P('dp', None, 'mp'), may hold values from -6 to 6
- errors: float32 [32, 256, 28672], P('dp', None, 'mp'), may hold values from -4 to 4
- q_init: float32 [28672, 32], P('mp'), may hold values from -6 to 6
Outputs:
- update: bfloat16 [256, 28672], P(None, 'mp')
- new_errors: float32 [32, 256, 28672], P('dp', None, 'mp')
- q_next: float32 [28672, 32], P('mp')
All inputs are finite; a program needn't handle non-finite values.
Results may differ from a plain program's by a relative error of at most 0.001.
Values sent between devices are 32-bit elements; how exact they have to be, the bound alone decides.
A program may use at most 64 MiB of HBM per device.

v0:
```python
import jax
import jax.numpy as jnp
from jax import lax
from jax.sharding import PartitionSpec as P


def orthonormal(p_sum):
    gram = jnp.dot(p_sum.T, p_sum, precision=lax.Precision.HIGHEST)
    lower = jnp.linalg.cholesky(gram)
    return jax.scipy.linalg.solve_triangular(lower, p_sum.T, lower=True).T


def body(grads, errors, q_init):
    merged = grads[0].astype(jnp.float32) + errors[0]
    p_local = jnp.dot(merged, q_init, precision=lax.Precision.HIGHEST)
    p_sum = lax.psum(p_local, ("dp", "mp"))
    p_hat = orthonormal(p_sum)
    replicas = lax.axis_size("dp")
    q_local = lax.dot_general(
        merged, p_hat, (((0,), (0,)), ((), ())), precision=lax.Precision.HIGHEST
    )
    q_next = lax.psum(q_local, "dp") / replicas
    recon = jnp.dot(p_hat, q_next.T, precision=lax.Precision.HIGHEST)
    update = recon.astype(jnp.bfloat16)
    new_errors = (merged - recon)[None]
    return (update, new_errors, q_next)


def solution(mesh):
    placed = (P("dp", None, "mp"), P("dp", None, "mp"), P("mp", None))
    return jax.shard_map(
        body,
        mesh=mesh,
        in_specs=placed,
        out_specs=(P(None, "mp"), P("dp", None, "mp"), P("mp", None)),
        check_vma=False,
    )
```

profile of v0, /device:TPU:8, one launch (start us, length us, event | category | flops | bytes accessed | tf_op | source)
XLA Modules:
  0.0 264.2 jit_solution(156344949375325960)
XLA Ops:
  7.2 0.0 copy-start
  7.2 0.0 copy-start.1
  7.2 0.0 all-reduce.2.cloned.1.call-start
  7.2 1.0 copy-done
  8.2 5.8 %fusion.2 = f32[256,32]{0,1:T(8,128)S(1)} fusion(f32[3584,32]{0,1:T(8,128)S(1)} %copy-done, f32[1,256,3584]{2,1,0:T(8,128)} %param.4, bf16[1,256,3584]{2,1,0:T(8,128)(2,1)} %param.3), kind=kOutput, calls=%fused_computation.3 | convolution fusion | flops 354156544 | bytes 5996544 | tf_op jit(solution)/shard_map/dot_general | solution.py:15
  14.0 78.7 %psum.14 = f32[256,32]{0,1:T(8,128)S(1)} all-reduce(f32[256,32]{0,1:T(8,128)S(1)} %fusion.2), channel_id=1, replica_groups=mesh['dp'=32,'mp'=8] {'dp','mp'}, use_global_device_ids=true, to_apply=%region_0.0 | all-reduce | flops 8192 | bytes 65536 | tf_op jit(solution)/shard_map/psum | solution.py:16
  92.8 0.2 fusion.9
  92.9 0.1 copy.6
  93.0 2.9 %cholesky.16 = f32[32,32]{1,0:T(8,128)S(1)} custom-call(f32[32,32]{1,0:T(8,128)S(1)} %fusion.8), custom_call_target="Cholesky" | custom-call | tf_op jit(solution)/shard_map/jit(cholesky)/cholesky | solution.py:9
  96.0 0.6 compare_reduce_fusion
  96.6 0.7 fusion.5
  97.3 2.4 custom-call.7
  99.7 0.2 fusion.6
  99.9 0.0 copy-done.1
  100.0 5.3 %fusion = f32[3584,32]{0,1:T(8,128)} fusion(f32[32,256]{1,0:T(8,128)S(1)} %fusion.6, f32[1,256,3584]{2,1,0:T(8,128)} %param.4, bf16[1,256,3584]{2,1,0:T(8,128)(2,1)S(1)} %copy-done.1), kind=kOutput, calls=%fused_computation.1 | convolution fusion | flops 354156544 | bytes 5996544 | tf_op jit(solution)/shard_map/dot_general | solution.py:19
  105.2 0.0 all-reduce.2.cloned.1.call-update
  105.2 144.5 %all-reduce.2.cloned.1.call-done = f32[3584,32]{0,1:T(8,128)} async-done(((f32[3584,32]{0,1:T(8,128)}), f32[3584,32]{0,1:T(8,128)}) %all-reduce.2.cloned.1.call-update) | async-done | bytes 458768 | tf_op jit(solution)/shard_map/psum | solution.py:22
  249.7 1.0 broadcast_multiply_fusion
  250.8 0.0 copy-start.2
  250.8 6.6 %fusion.4 = (f32[1,256,3584]{2,1,0:T(8,128)}, bf16[256,3584]{1,0:T(8,128)(2,1)}) fusion(f32[1,256,3584]{2,1,0:T(8,128)} %param.4, bf16[1,256,3584]{2,1,0:T(8,128)(2,1)S(1)} %copy-done.1, f32[32,256]{1,0:T(8,128)S(1)} %fusion.6, f32[3584,32]{0,1:T(8,128)S(1)} %broadcast_multiply_fusion), kind=kOutput, calls=%fused_computation.5 | convolution fusion | flops 355991552 | bytes 11501568 | tf_op jit(solution)/shard_map/dot_general | solution.py:23
  257.4 0.0 copy-done.2
  (2 shorter events, 0.0 us)
Async XLA Ops:
  7.2 1.0 copy-start
  7.2 92.8 %copy-start.1 = (bf16[1,256,3584]{2,1,0:T(8,128)(2,1)S(1)}, bf16[1,256,3584]{2,1,0:T(8,128)(2,1)}, u32[]{:S(2)}) copy-start(bf16[1,256,3584]{2,1,0:T(8,128)(2,1)} %param.3) | copy-start | bytes 5505028
  7.2 242.5 %all-reduce.2.cloned.1.call-start = ((), (), s32[]{:S(2)}) async-start(), calls=%async_computation | async-start | bytes 917504 | tf_op jit(solution)/shard_map/psum | solution.py:22
  250.8 6.6 %copy-start.2 = (f32[3584,32]{0,1:T(8,128)}, f32[3584,32]{0,1:T(8,128)S(1)}, u32[]{:S(2)}) copy-start(f32[3584,32]{0,1:T(8,128)S(1)} %broadcast_multiply_fusion) | copy-start | bytes 1376260
Sparse Core Ops, SparseCore 0:
  105.4 144.3 all-reduce.1
where the time goes:
time: 265 us; the launch traced here: 264 us
  waiting for transfers between devices  144 us (54%)
  blocking collectives  78.7 us (30%)
  matrix products  18.1 us (7%)
  between operations  14.1 us (5%)
  other arithmetic  7.74 us (3%)
    psum x1, waiting for transfers between devices, body(): q_next = lax.psum(q_local, 'dp') / replicas  144 us
    psum x1, blocking collectives, body(): p_sum = lax.psum(p_local, ('dp', 'mp'))  78.7 us
    dot_general x1, matrix products, body(): recon = jnp.dot(p_hat, q_next.T, precision=lax.Precision.HIGHEST)  6.6 us
    dot_general x1, matrix products, body(): p_local = jnp.dot(merged, q_init, precision=lax.Precision.HIGHEST)  5.81 us
  transfers between devices with their start and end apart: 1, of which 1 were waited for; matrix products, arithmetic and copies ran while one was open for 0% of the time, Pallas kernels for 0%

commit v1 on v0

v1 whole, which is shorter than its diff:
```python
import functools

import jax
import jax.numpy as jnp
from jax import lax
from jax.experimental import pallas as pl
from jax.experimental.pallas import tpu as pltpu
from jax.sharding import PartitionSpec as P

MESH = pl.DeviceIdType.MESH
HIGHEST = lax.Precision.HIGHEST
F32 = jnp.float32
BF16 = jnp.bfloat16

NZ, NX, NMP = 8, 4, 8
ROWS, RANK = 256, 32
VMEM = pl.BlockSpec(memory_space=pltpu.VMEM)
ANY = pl.BlockSpec(memory_space=pl.ANY)


def ring_hops(offset, size):
    return min(offset, size - offset)


Z_OFFSETS = sorted(range(1, NZ), key=lambda d: -ring_hops(d, NZ))
X_OFFSETS = sorted(range(1, NX), key=lambda d: -ring_hops(d, NX))
DP_OFFSETS = sorted(
    ((dz, dx) for dz in range(NZ) for dx in range(NX) if dz or dx),
    key=lambda d: -(ring_hops(d[0], NZ) + ring_hops(d[1], NX)),
)
MP_OFFSETS = [4, 5, 2, 6, 3, 7, 1]


def split(value):
    high = value.astype(BF16)
    return high, (value - high.astype(F32)).astype(BF16)


def dot_t(a, b):
    return lax.dot_general(a, b, (((1,), (1,)), ((), ())), preferred_element_type=F32)


def inverse_factor(gram):
    rows = lax.broadcasted_iota(jnp.int32, (RANK, 4 * RANK), 0)
    lanes = lax.broadcasted_iota(jnp.int32, (RANK, 4 * RANK), 1)
    work = jnp.where(lanes == rows + RANK, 1.0, 0.0)
    work = work + jnp.concatenate([gram, jnp.zeros((RANK, 3 * RANK), F32)], axis=1)
    for k in range(RANK):
        row = work[k : k + 1, :]
        pivot = work[k : k + 1, k : k + 1]
        column = work[:, k : k + 1]
        scale = lax.rsqrt(pivot)
        row = row * scale
        step = work - (column * scale) * row
        below = rows > k
        work = jnp.where(below, step, jnp.where(rows == k, row, work))
    return work[:, RANK : 2 * RANK]


def reduce_kernel(
    g_hbm, e_hbm, qt_hbm, q_out, inv_out, phat_out,
    g_v, e_v, qt_v, high_v, low_v, p_loc, p_rs, p_ar, p_all,
    x_src, x_buf, z_src, z_buf, ag,
    load_sem, p_send, p_recv, x_send, x_recv, z_send, z_recv, ag_send, agz_recv, agx_recv,
):
    dp, mp = lax.axis_index("dp"), lax.axis_index("mp")
    z, x = dp // NX, lax.rem(dp, NX)
    width = g_v.shape[2]

    def z_peer(d):
        return lax.rem(z + d, NZ)

    def x_peer(d):
        return lax.rem(x + d, NX)

    def dp_peer(dz, dx):
        return z_peer(dz) * NX + x_peer(dx)

    def mp_peer(d):
        return lax.rem(mp + d, NMP)

    def send(src, dst, send_sem, recv_sem, dp_to, mp_to):
        pltpu.make_async_remote_copy(
            src_ref=src, dst_ref=dst, send_sem=send_sem, recv_sem=recv_sem,
            device_id=(dp_to, mp_to), device_id_type=MESH,
        ).start()

    def wait_bytes(ref, sem):
        pltpu.make_async_copy(ref, ref, sem).wait()

    loads = []
    for i in range(NX):
        cols = pl.ds(i * width, width)
        three = [
            pltpu.make_async_copy(g_hbm.at[0, :, cols], g_v.at[i], load_sem.at[0, i]),
            pltpu.make_async_copy(e_hbm.at[0, :, cols], e_v.at[i], load_sem.at[1, i]),
            pltpu.make_async_copy(qt_hbm.at[:, cols], qt_v.at[i], load_sem.at[2, i]),
        ]
        for copy in three:
            copy.start()
        loads.append(three)

    barrier = pltpu.get_barrier_semaphore()
    for dz, dx in DP_OFFSETS:
        pl.semaphore_signal(barrier, inc=1, device_id=(dp_peer(dz, dx), mp), device_id_type=MESH)
    for d in MP_OFFSETS:
        pl.semaphore_signal(barrier, inc=1, device_id=(dp, mp_peer(d)), device_id_type=MESH)

    p_part = jnp.zeros((ROWS, 2 * RANK), F32)
    for i in range(NX):
        for copy in loads[i]:
            copy.wait()
        high, low = split(g_v[i].astype(F32) + e_v[i])
        high_v[i] = high
        low_v[i] = low
        q_both = jnp.concatenate(split(qt_v[i]), axis=0)
        p_part += dot_t(high, q_both) + dot_t(low, q_both)
    p_t = (p_part[:, :RANK] + p_part[:, RANK:]).T
    for t in range(NMP):
        p_loc[t] = p_t[8 * (t % 4) : 8 * (t % 4) + 8, 128 * (t // 4) : 128 * (t // 4) + 128]

    pl.semaphore_wait(barrier, len(DP_OFFSETS) + len(MP_OFFSETS))

    for d in MP_OFFSETS:
        to = mp_peer(d)
        send(p_loc.at[to], p_rs.at[mp], p_send.at[0], p_recv.at[0], dp, to)
    p_rs[mp] = p_loc[mp]
    wait_bytes(p_rs.at[pl.ds(0, NMP - 1)], p_recv.at[0])
    p_ar[dp] = jnp.sum(p_rs[...], axis=0)
    for dz, dx in DP_OFFSETS:
        send(p_ar.at[dp], p_ar.at[dp], p_send.at[1], p_recv.at[1], dp_peer(dz, dx), mp)
    wait_bytes(p_ar.at[pl.ds(0, NZ * NX - 1)], p_recv.at[1])
    p_all[mp] = jnp.sum(p_ar[...], axis=0)
    for d in MP_OFFSETS:
        send(p_all.at[mp], p_all.at[mp], p_send.at[2], p_recv.at[2], dp, mp_peer(d))
    wait_bytes(p_all.at[pl.ds(0, NMP - 1)], p_recv.at[2])
    p_t = jnp.concatenate(
        [
            jnp.concatenate([p_all[t] for t in range(4)], axis=0),
            jnp.concatenate([p_all[t] for t in range(4, 8)], axis=0),
        ],
        axis=1,
    )

    p_high, p_low = split(p_t)
    p_both = jnp.concatenate([p_high, p_low], axis=0)
    for d in X_OFFSETS + [0]:
        to = x_peer(d)
        first = jnp.dot(p_both, high_v[to], preferred_element_type=F32)
        second = jnp.dot(p_high, low_v[to], preferred_element_type=F32)
        block = first[:RANK] + first[RANK:] + second
        if d:
            x_src[to] = block
            send(x_src.at[to], x_buf.at[x], x_send, x_recv, z * NX + to, mp)
        else:
            x_buf[x] = block

    gram = lax.dot_general(
        p_t, p_t, (((1,), (1,)), ((), ())), precision=HIGHEST, preferred_element_type=F32
    )
    inverse = inverse_factor(gram)
    inv_out[...] = inverse
    phat_out[...] = jnp.dot(inverse, p_t, precision=HIGHEST, preferred_element_type=F32).T

    wait_bytes(x_buf.at[pl.ds(0, NX - 1)], x_recv)
    block = jnp.sum(x_buf[...], axis=0)
    rows = RANK // NZ
    for i in range(NZ):
        z_src[i] = block[i * rows : (i + 1) * rows]
    for d in Z_OFFSETS:
        to = z_peer(d)
        send(z_src.at[to], z_buf.at[z], z_send, z_recv, to * NX + x, mp)
    z_buf[z] = z_src[z]
    wait_bytes(z_buf.at[pl.ds(0, NZ - 1)], z_recv)
    ag[x, z] = jnp.sum(z_buf[...], axis=0)

    for d in Z_OFFSETS:
        send(ag.at[x, z], ag.at[x, z], ag_send, agz_recv.at[z], z_peer(d) * NX + x, mp)
    for d in [0] + Z_OFFSETS[::-1]:
        at = z_peer(d)
        if d:
            wait_bytes(ag.at[x, at], agz_recv.at[at])
        for dx in X_OFFSETS:
            send(ag.at[x, at], ag.at[x, at], ag_send, agx_recv, z * NX + x_peer(dx), mp)
    wait_bytes(ag.at[pl.ds(0, NX - 1)], agx_recv)
    for i in range(NX):
        q_out[:, i * width : (i + 1) * width] = jnp.concatenate(
            [ag[i, j] for j in range(NZ)], axis=0
        )

    wait_bytes(p_rs.at[pl.ds(0, NMP - 1)], p_send.at[0])
    wait_bytes(p_ar.at[pl.ds(0, NZ * NX - 1)], p_send.at[1])
    wait_bytes(p_all.at[pl.ds(0, NMP - 1)], p_send.at[2])
    wait_bytes(x_buf.at[pl.ds(0, NX - 1)], x_send)
    wait_bytes(z_buf.at[pl.ds(0, NZ - 1)], z_send)
    wait_bytes(ag.at[pl.ds(0, NX - 1)], ag_send)
    wait_bytes(ag.at[0, pl.ds(0, NZ - 1)], ag_send)


def finish_kernel(replicas, g_ref, e_ref, q_ref, inv_ref, phat_ref, u_ref, n_ref, q_out):
    q_next = jnp.dot(inv_ref[...], q_ref[...], precision=HIGHEST, preferred_element_type=F32)
    q_next = q_next * (1.0 / replicas)
    q_out[...] = q_next
    p_high, p_low = split(phat_ref[...])
    q_high, q_low = split(q_next)
    left = jnp.concatenate([p_high, p_low, p_high, p_low], axis=1)
    right = jnp.concatenate([q_high, q_high, q_low, q_low], axis=0)
    recon = jnp.dot(left, right, preferred_element_type=F32)
    u_ref[...] = recon.astype(BF16)
    n_ref[0] = g_ref[0].astype(F32) + e_ref[0] - recon


def body(grads, errors, q_init):
    columns = grads.shape[2]
    width = columns // NX
    piece = RANK // NZ
    dma = pltpu.SemaphoreType.DMA
    q_sum, inverse, p_hat = pl.pallas_call(
        reduce_kernel,
        out_shape=(
            jax.ShapeDtypeStruct((RANK, columns), F32),
            jax.ShapeDtypeStruct((RANK, RANK), F32),
            jax.ShapeDtypeStruct((ROWS, RANK), F32),
        ),
        in_specs=[ANY] * 3,
        out_specs=[VMEM] * 3,
        scratch_shapes=[
            pltpu.VMEM((NX, ROWS, width), BF16),
            pltpu.VMEM((NX, ROWS, width), F32),
            pltpu.VMEM((NX, RANK, width), F32),
            pltpu.VMEM((NX, ROWS, width), BF16),
            pltpu.VMEM((NX, ROWS, width), BF16),
            pltpu.VMEM((NMP, 8, 128), F32),
            pltpu.VMEM((NMP, 8, 128), F32),
            pltpu.VMEM((NZ * NX, 8, 128), F32),
            pltpu.VMEM((NMP, 8, 128), F32),
            pltpu.VMEM((NX, RANK, width), F32),
            pltpu.VMEM((NX, RANK, width), F32),
            pltpu.VMEM((NZ, piece, width), F32),
            pltpu.VMEM((NZ, piece, width), F32),
            pltpu.VMEM((NX, NZ, piece, width), F32),
            dma((3, NX)),
            dma((3,)),
            dma((3,)),
            dma,
            dma,
            dma,
            dma,
            dma,
            dma((NZ,)),
            dma,
        ],
        compiler_params=pltpu.CompilerParams(
            collective_id=0, has_side_effects=True, vmem_limit_bytes=40 << 20
        ),
        name="reduce",
    )(grads, errors, q_init.T)

    block = 512
    update, new_errors, q_next = pl.pallas_call(
        functools.partial(finish_kernel, lax.axis_size("dp")),
        grid=(columns // block,),
        out_shape=(
            jax.ShapeDtypeStruct((ROWS, columns), BF16),
            jax.ShapeDtypeStruct((1, ROWS, columns), F32),
            jax.ShapeDtypeStruct((RANK, columns), F32),
        ),
        in_specs=[
            pl.BlockSpec((1, ROWS, block), lambda j: (0, 0, j)),
            pl.BlockSpec((1, ROWS, block), lambda j: (0, 0, j)),
            pl.BlockSpec((RANK, block), lambda j: (0, j)),
            pl.BlockSpec((RANK, RANK), lambda j: (0, 0)),
            pl.BlockSpec((ROWS, RANK), lambda j: (0, 0)),
        ],
        out_specs=(
            pl.BlockSpec((ROWS, block), lambda j: (0, j)),
            pl.BlockSpec((1, ROWS, block), lambda j: (0, 0, j)),
            pl.BlockSpec((RANK, block), lambda j: (0, j)),
        ),
        compiler_params=pltpu.CompilerParams(vmem_limit_bytes=32 << 20),
        name="finish",
    )(grads, errors, q_sum, inverse, p_hat)
    return (update, new_errors, q_next.T)


def solution(mesh):
    placed = (P("dp", None, "mp"), P("dp", None, "mp"), P("mp", None))
    return jax.shard_map(
        body,
        mesh=mesh,
        in_specs=placed,
        out_specs=(P(None, "mp"), P("dp", None, "mp"), P("mp", None)),
        check_vma=False,
    )
```

time: 265 us -> 56.6 us (0.21)
  waiting for transfers between devices: 144 us -> 0 us
  blocking collectives: 78.7 us -> 0 us
  Pallas kernels: 0 us -> 50.7 us
  matrix products: 18.1 us -> 0 us
  between operations: 14.1 us -> 0.65 us
  other arithmetic: 7.74 us -> 0 us
  local copies, waits for them, and re-layouts: 1.04 us -> 4.55 us
    psum x1 -> x0, waiting for transfers between devices: 144 us -> none  [body(): q_next = lax.psum(q_local, 'dp') / replicas]
    psum x1 -> x0, blocking collectives: 78.7 us -> none  [body(): p_sum = lax.psum(p_local, ('dp', 'mp'))]
    pallas_call x0 -> x2, Pallas kernels: none -> 50.7 us  [the longest x1 45.2 us: body(): pl.pallas_call(reduce_kernel, out_shape=(jax.ShapeDtypeStruct((RANK, colu...]
    dot_general x4 -> x0, matrix products: 17.8 us -> none  [the longest x1 6.6 us: body(): recon = jnp.dot(p_hat, q_next.T, precision=lax.Precision.HIGHEST)]
    another operation x5 -> x0, other arithmetic: 6.68 us -> none  [the longest x3 3.6 us: orthonormal(): lower = jnp.linalg.cholesky(gram)]
    unnamed x6, local copies, waits for them, and re-layouts: 0.97 us -> 4.55 us
  transfers between devices with their start and end apart: 1 -> 0, of which waited for: 1 -> 0; matrix products, arithmetic and copies ran while one was open for 0% -> 0% of each run, Pallas kernels for 0% -> 0%
where the time goes in v1:
time: 56.6 us; the launch traced here: 55.9 us
  Pallas kernels  50.7 us (90%)
  local copies, waits for them, and re-layouts  4.55 us (8%)
  between operations  0.65 us (1%)
    pallas_call x1, Pallas kernels, body(): pl.pallas_call(reduce_kernel, out_shape=(jax.ShapeDtypeStruct((RANK, colu...  45.2 us
    pallas_call x1, Pallas kernels, body(): pl.pallas_call(functools.partial(finish_kernel, lax.axis_size('dp')), gri...  5.48 us
    unnamed x6, local copies, waits for them, and re-layouts  4.55 us

profile of v1, /device:TPU:8, one launch (start us, length us, event | category | flops | bytes accessed | tf_op | source)
XLA Modules:
  0.0 55.9 jit_solution(9797411711300232535)
XLA Ops:
  0.6 0.0 copy-start
  0.6 2.0 %copy-done = f32[1,256,3584]{2,1,0:T(8,128)S(1)} copy-done((f32[1,256,3584]{2,1,0:T(8,128)S(1)}, f32[1,256,3584]{2,1,0:T(8,128)}, u32[]{:S(2)}) %copy-start) | copy-done | bytes 3670040
  2.7 0.0 copy-start.1
  2.7 1.5 %copy-done.1 = bf16[1,256,3584]{2,1,0:T(8,128)(2,1)S(1)} copy-done((bf16[1,256,3584]{2,1,0:T(8,128)(2,1)S(1)}, bf16[1,256,3584]{2,1,0:T(8,128)(2,1)}, u32[]{:S(2)}) %copy-start.1) | copy-done | bytes 1835032
  4.2 0.0 copy-start.2
  4.2 1.0 %copy-done.2 = f32[3584,32]{0,1:T(8,128)S(1)} copy-done((f32[3584,32]{0,1:T(8,128)S(1)}, f32[3584,32]{0,1:T(8,128)}, u32[]{:S(2)}) %copy-start.2) | copy-done | bytes 458776
  5.2 45.2 %reduce.1 = (f32[32,3584]{1,0:T(8,128)S(1)}, f32[32,32]{1,0:T(8,128)S(1)}, f32[256,32]{1,0:T(8,128)S(1)}) custom-call(bf16[1,256,3584]{2,1,0:T(8,128)(2,1)S(1)} %copy-done.1, f32[1,256,3584]{2,1,0:T(8,128)S(1)} %copy-done, f32[32,3584]{1,0:T(8,128)S(1)} %bitcast.2), custom_call_target="tpu_custom_call" | custom-call | tf_op jit(solution)/shard_map/reduce/pallas_call | solution.py:218
  50.4 5.5 %finish.1 = (bf16[256,3584]{1,0:T(8,128)(2,1)}, f32[1,256,3584]{2,1,0:T(8,128)}, f32[32,3584]{1,0:T(8,128)}) custom-call(bf16[1,256,3584]{2,1,0:T(8,128)(2,1)S(1)} %copy-done.1, f32[1,256,3584]{2,1,0:T(8,128)S(1)} %copy-done, f32[32,3584]{1,0:T(8,128)S(1)} %get-tuple-element.9.q_ref, f32[32,32]{1,0:T(8,128)S(1)} %get-tuple-element.10.inv_ref, ...), custom_call_target="tpu_custom_call" | custom-call | tf_op jit(solution)/shard_map/finish/pallas_call | solution.py:260
Async XLA Ops:
  0.6 2.0 %copy-start = (f32[1,256,3584]{2,1,0:T(8,128)S(1)}, f32[1,256,3584]{2,1,0:T(8,128)}, u32[]{:S(2)}) copy-start(f32[1,256,3584]{2,1,0:T(8,128)} %e_ref.1) | copy-start | bytes 11010052
  2.7 1.5 %copy-start.1 = (bf16[1,256,3584]{2,1,0:T(8,128)(2,1)S(1)}, bf16[1,256,3584]{2,1,0:T(8,128)(2,1)}, u32[]{:S(2)}) copy-start(bf16[1,256,3584]{2,1,0:T(8,128)(2,1)} %g_ref.1) | copy-start | bytes 5505028
  4.2 1.0 %copy-start.2 = (f32[3584,32]{0,1:T(8,128)S(1)}, f32[3584,32]{0,1:T(8,128)}, u32[]{:S(2)}) copy-start(f32[3584,32]{0,1:T(8,128)} %param.5) | copy-start | bytes 1376260

commit v2 on v1

v2 whole, which is shorter than its diff:
```python
import functools

import jax
import jax.numpy as jnp
from jax import lax
from jax.experimental import pallas as pl
from jax.experimental.pallas import tpu as pltpu
from jax.sharding import PartitionSpec as P

MESH = pl.DeviceIdType.MESH
HIGHEST = lax.Precision.HIGHEST
F32 = jnp.float32
BF16 = jnp.bfloat16

NZ, NX, NMP = 8, 4, 8
ROWS, RANK = 256, 32
VMEM = pl.BlockSpec(memory_space=pltpu.VMEM)
HBM = pl.BlockSpec(memory_space=pltpu.HBM)


def around(i, size):
    half = (i + 1) // 2
    return lax.rem(size // 2 + jnp.where(lax.rem(i, 2) == 0, half, size - half), size)


def split(value):
    high = value.astype(BF16)
    return high, (value - high.astype(F32)).astype(BF16)


def split3(value):
    high = value.astype(BF16)
    middle, low = split(value - high.astype(F32))
    return high, middle, low


def stack_left(value):
    h, m, l = split3(value)
    return jnp.concatenate([h, h, m, h, m, l], axis=1)


def stack_right(value):
    h, m, l = split3(value)
    return jnp.concatenate([h, m, h, l, m, h], axis=0)


def dot_t(a, b):
    return lax.dot_general(a, b, (((1,), (1,)), ((), ())), preferred_element_type=F32)


def inverse_factor(gram):
    rows = lax.broadcasted_iota(jnp.int32, (RANK, 4 * RANK), 0)
    lanes = lax.broadcasted_iota(jnp.int32, (RANK, 4 * RANK), 1)
    work = jnp.where(lanes == rows + RANK, 1.0, 0.0)
    work = work + jnp.concatenate([gram, jnp.zeros((RANK, 3 * RANK), F32)], axis=1)
    for k in range(RANK):
        row = work[k : k + 1, :]
        pivot = work[k : k + 1, k : k + 1]
        column = work[:, k : k + 1]
        scale = lax.rsqrt(pivot)
        row = row * scale
        step = work - (column * scale) * row
        below = rows > k
        work = jnp.where(below, step, jnp.where(rows == k, row, work))
    return work[:, RANK : 2 * RANK]


def reduce_kernel(
    g_hbm, e_hbm, qt_hbm, merged_out, q_out, inv_out, phat_out,
    g_v, e_v, qt_v, high_v, low_v, p_acc, p_loc, p_rs, p_ar, p_all,
    x_src, x_buf, z_src, z_buf, ag,
    load_sem, p_send, p_recv, x_send, x_recv, z_send, z_recv, ag_send, agz_recv, agx_recv,
):
    dp, mp = lax.axis_index("dp"), lax.axis_index("mp")
    z, x = dp // NX, lax.rem(dp, NX)
    y, core = mp // 2, lax.rem(mp, 2)
    width = g_v.shape[2]
    n_dp = NZ * NX

    def z_peer(i):
        return lax.rem(z + around(i, NZ), NZ)

    def x_peer(i):
        return lax.rem(x + around(i, NX), NX)

    def dp_peer(i):
        return z_peer(i // NX) * NX + x_peer(lax.rem(i, NX))

    def mp_peer(i):
        return lax.rem(y + around(i // 2, NMP // 2), NMP // 2) * 2 + lax.rem(core + i + 1, 2)

    def each(n, act):
        lax.fori_loop(0, n, lambda i, c: (act(i), c)[1], 0)

    def send(src, dst, send_sem, recv_sem, dp_to, mp_to):
        pltpu.make_async_remote_copy(
            src_ref=src, dst_ref=dst, send_sem=send_sem, recv_sem=recv_sem,
            device_id=(dp_to, mp_to), device_id_type=MESH,
        ).start()

    def wait_bytes(ref, sem):
        pltpu.make_async_copy(ref, ref, sem).wait()

    def loads(i):
        cols = pl.ds(pl.multiple_of(i * width, 128), width)
        return (
            pltpu.make_async_copy(qt_hbm.at[:, cols], qt_v.at[i], load_sem.at[2, i]),
            pltpu.make_async_copy(g_hbm.at[0, :, cols], g_v.at[i], load_sem.at[0, i]),
            pltpu.make_async_copy(e_hbm.at[0, :, cols], e_v.at[i], load_sem.at[1, i]),
        )

    @functools.partial(each, NX)
    def _(i):
        for copy in loads(i):
            copy.start()

    barrier = pltpu.get_barrier_semaphore()

    @functools.partial(each, n_dp - 1)
    def _(i):
        pl.semaphore_signal(barrier, inc=1, device_id=(dp_peer(i), mp), device_id_type=MESH)

    @functools.partial(each, NMP - 1)
    def _(i):
        pl.semaphore_signal(barrier, inc=1, device_id=(dp, mp_peer(i)), device_id_type=MESH)

    drain = []

    p_acc[...] = jnp.zeros_like(p_acc)

    @functools.partial(each, NX)
    def _(i):
        for copy in loads(i):
            copy.wait()
        merged = g_v[i].astype(F32) + e_v[i]
        merged_out[i] = merged
        high, low = split(merged)
        high_v[i] = high
        low_v[i] = low
        q_both = jnp.concatenate(split(qt_v[i]), axis=0)
        p_acc[...] += dot_t(high, q_both) + dot_t(low, q_both)

    p_t = (p_acc[:, :RANK] + p_acc[:, RANK:]).T
    for t in range(NMP):
        p_loc[t] = p_t[8 * (t % 4) : 8 * (t % 4) + 8, 128 * (t // 4) : 128 * (t // 4) + 128]

    pl.semaphore_wait(barrier, n_dp - 1 + NMP - 1)

    @functools.partial(each, NMP - 1)
    def _(i):
        to = mp_peer(i)
        send(p_loc.at[to], p_rs.at[mp], p_send.at[0], p_recv.at[0], dp, to)

    drain.append((p_rs.at[pl.ds(0, NMP - 1)], p_send.at[0]))
    p_rs[mp] = p_loc[mp]
    wait_bytes(p_rs.at[pl.ds(0, NMP - 1)], p_recv.at[0])
    p_ar[dp] = jnp.sum(p_rs[...], axis=0)

    @functools.partial(each, n_dp - 1)
    def _(i):
        send(p_ar.at[dp], p_ar.at[dp], p_send.at[1], p_recv.at[1], dp_peer(i), mp)

    drain.append((p_ar.at[pl.ds(0, n_dp - 1)], p_send.at[1]))
    wait_bytes(p_ar.at[pl.ds(0, n_dp - 1)], p_recv.at[1])
    p_all[mp] = jnp.sum(p_ar[...], axis=0)

    @functools.partial(each, NMP - 1)
    def _(i):
        send(p_all.at[mp], p_all.at[mp], p_send.at[2], p_recv.at[2], dp, mp_peer(i))

    drain.append((p_all.at[pl.ds(0, NMP - 1)], p_send.at[2]))
    wait_bytes(p_all.at[pl.ds(0, NMP - 1)], p_recv.at[2])
    p_t = jnp.concatenate(
        [
            jnp.concatenate([p_all[t] for t in range(4)], axis=0),
            jnp.concatenate([p_all[t] for t in range(4, 8)], axis=0),
        ],
        axis=1,
    )

    p_both = jnp.concatenate(split(p_t), axis=0)

    @functools.partial(each, NX)
    def _(i):
        to = x_peer(i)
        both = jnp.dot(p_both, high_v[to], preferred_element_type=F32)
        both += jnp.dot(p_both, low_v[to], preferred_element_type=F32)
        x_src[to] = both[:RANK] + both[RANK:]

        @pl.when(i < NX - 1)
        def _():
            send(x_src.at[to], x_buf.at[x], x_send, x_recv, z * NX + to, mp)

    drain.append((x_buf.at[pl.ds(0, NX - 1)], x_send))
    x_buf[x] = x_src[x]

    gram = lax.dot_general(
        p_t, p_t, (((1,), (1,)), ((), ())), precision=HIGHEST, preferred_element_type=F32
    )
    inverse = inverse_factor(gram)
    inv_out[...] = stack_left(inverse)
    phat_out[...] = stack_left(
        jnp.dot(inverse, p_t, precision=HIGHEST, preferred_element_type=F32).T
    )

    wait_bytes(x_buf.at[pl.ds(0, NX - 1)], x_recv)
    block = jnp.sum(x_buf[...], axis=0)
    rows = RANK // NZ
    for i in range(NZ):
        z_src[i] = block[i * rows : (i + 1) * rows]

    @functools.partial(each, NZ - 1)
    def _(i):
        to = z_peer(i)
        send(z_src.at[to], z_buf.at[z], z_send, z_recv, to * NX + x, mp)

    drain.append((z_buf.at[pl.ds(0, NZ - 1)], z_send))
    z_buf[z] = z_src[z]
    wait_bytes(z_buf.at[pl.ds(0, NZ - 1)], z_recv)
    ag[x, z] = jnp.sum(z_buf[...], axis=0)

    @functools.partial(each, NZ - 1)
    def _(i):
        send(ag.at[x, z], ag.at[x, z], ag_send, agz_recv.at[z], z_peer(i) * NX + x, mp)

    @functools.partial(each, NZ)
    def _(i):
        at = z_peer(NZ - 1 - i)

        @pl.when(i > 0)
        def _():
            wait_bytes(ag.at[x, at], agz_recv.at[at])

        @functools.partial(each, NX - 1)
        def _(j):
            send(ag.at[x, at], ag.at[x, at], ag_send, agx_recv, z * NX + x_peer(j), mp)

    drain.append((ag.at[pl.ds(0, NX - 1)], ag_send))
    drain.append((ag.at[0, pl.ds(0, NZ - 1)], ag_send))
    wait_bytes(ag.at[pl.ds(0, NX - 1)], agx_recv)
    for i in range(NX):
        q_out[i] = jnp.concatenate([ag[i, j] for j in range(NZ)], axis=0)

    for ref, sem in drain:
        wait_bytes(ref, sem)


def finish_kernel(
    replicas, merged_ref, q_ref, inv_ref, phat_ref, u_hbm, n_hbm, q_hbm, u_v, n_v, q_v, sems
):
    blocks, _, width = merged_ref.shape
    half = ROWS // 2

    def block(i, carry):
        cols = pl.ds(pl.multiple_of(i * width, 128), width)
        q_next = jnp.dot(inv_ref[...], stack_right(q_ref[i]), preferred_element_type=F32)
        q_next = q_next * (1.0 / replicas)
        q_v[i] = q_next
        pltpu.make_async_copy(q_v.at[i], q_hbm.at[:, cols], sems.at[0]).start()
        right = stack_right(q_next)
        for h in range(2):
            rows = slice(h * half, (h + 1) * half)
            at = pl.ds(h * half, half)
            recon = jnp.dot(phat_ref[rows], right, preferred_element_type=F32)
            n_v[i, rows] = merged_ref[i, rows] - recon
            pltpu.make_async_copy(n_v.at[i, at], n_hbm.at[0, at, cols], sems.at[1]).start()
            u_v[i, rows] = recon.astype(BF16)
            pltpu.make_async_copy(u_v.at[i, at], u_hbm.at[at, cols], sems.at[2]).start()
        return carry

    lax.fori_loop(0, blocks, block, 0)
    for ref, sem in ((q_v, sems.at[0]), (n_v, sems.at[1]), (u_v, sems.at[2])):
        pltpu.make_async_copy(ref, ref, sem).wait()


def body(grads, errors, q_init):
    columns = grads.shape[2]
    width = columns // NX
    piece = RANK // NZ
    dma = pltpu.SemaphoreType.DMA
    held = pl.pallas_call(
        reduce_kernel,
        out_shape=(
            jax.ShapeDtypeStruct((NX, ROWS, width), F32),
            jax.ShapeDtypeStruct((NX, RANK, width), F32),
            jax.ShapeDtypeStruct((RANK, 6 * RANK), BF16),
            jax.ShapeDtypeStruct((ROWS, 6 * RANK), BF16),
        ),
        in_specs=[HBM] * 3,
        out_specs=[VMEM] * 4,
        scratch_shapes=[
            pltpu.VMEM((NX, ROWS, width), BF16),
            pltpu.VMEM((NX, ROWS, width), F32),
            pltpu.VMEM((NX, RANK, width), F32),
            pltpu.VMEM((NX, ROWS, width), BF16),
            pltpu.VMEM((NX, ROWS, width), BF16),
            pltpu.VMEM((ROWS, 2 * RANK), F32),
            pltpu.VMEM((NMP, 8, 128), F32),
            pltpu.VMEM((NMP, 8, 128), F32),
            pltpu.VMEM((NZ * NX, 8, 128), F32),
            pltpu.VMEM((NMP, 8, 128), F32),
            pltpu.VMEM((NX, RANK, width), F32),
            pltpu.VMEM((NX, RANK, width), F32),
            pltpu.VMEM((NZ, piece, width), F32),
            pltpu.VMEM((NZ, piece, width), F32),
            pltpu.VMEM((NX, NZ, piece, width), F32),
            dma((3, NX)),
            dma((3,)),
            dma((3,)),
            dma,
            dma,
            dma,
            dma,
            dma,
            dma((NZ,)),
            dma,
        ],
        compiler_params=pltpu.CompilerParams(
            collective_id=0, has_side_effects=True, vmem_limit_bytes=40 << 20
        ),
        name="reduce",
    )(*(pltpu.with_memory_space_constraint(a, pltpu.HBM) for a in (grads, errors, q_init.T)))

    update, new_errors, q_next = pl.pallas_call(
        functools.partial(finish_kernel, lax.axis_size("dp")),
        out_shape=(
            jax.ShapeDtypeStruct((ROWS, columns), BF16),
            jax.ShapeDtypeStruct((1, ROWS, columns), F32),
            jax.ShapeDtypeStruct((RANK, columns), F32),
        ),
        in_specs=[VMEM] * 4,
        out_specs=[HBM] * 3,
        scratch_shapes=[
            pltpu.VMEM((NX, ROWS, width), BF16),
            pltpu.VMEM((NX, ROWS, width), F32),
            pltpu.VMEM((NX, RANK, width), F32),
            dma((3,)),
        ],
        compiler_params=pltpu.CompilerParams(vmem_limit_bytes=32 << 20),
        name="finish",
    )(*held)
    return (update, new_errors, q_next.T)


def solution(mesh):
    placed = (P("dp", None, "mp"), P("dp", None, "mp"), P("mp", None))
    return jax.shard_map(
        body,
        mesh=mesh,
        in_specs=placed,
        out_specs=(P(None, "mp"), P("dp", None, "mp"), P("mp", None)),
        check_vma=False,
    )
```

time: 56.6 us -> 48.8 us (0.86)
  local copies, waits for them, and re-layouts: 4.55 us -> 0 us
  Pallas kernels: 50.7 us -> 47.7 us
    unnamed x6 -> x0, local copies, waits for them, and re-layouts: 4.55 us -> none
    pallas_call x2, Pallas kernels: 50.7 us -> 47.7 us  [the longest x1 44.8 us: body(): pl.pallas_call(reduce_kernel, out_shape=(jax.ShapeDtypeStruct((NX, ROWS,...]
where the time goes in v2:
time: 48.8 us; the launch traced here: 48.3 us
  Pallas kernels  47.7 us (98%)
  between operations  0.64 us (1%)
    pallas_call x1, Pallas kernels, body(): pl.pallas_call(reduce_kernel, out_shape=(jax.ShapeDtypeStruct((NX, ROWS,...  44.8 us
    pallas_call x1, Pallas kernels, body(): pl.pallas_call(functools.partial(finish_kernel, lax.axis_size('dp')), out...  2.9 us

profile of v2, /device:TPU:8, one launch (start us, length us, event | category | flops | bytes accessed | tf_op | source)
XLA Modules:
  0.0 48.3 jit_solution(4654310777161323897)
XLA Ops:
  0.6 44.8 %reduce.1 = (f32[4,256,896]{2,1,0:T(8,128)S(1)}, f32[4,32,896]{2,1,0:T(8,128)S(1)}, bf16[32,192]{1,0:T(8,128)(2,1)S(1)}, bf16[256,192]{1,0:T(8,128)(2,1)S(1)}) custom-call(bf16[1,256,3584]{2,1,0:T(8,128)(2,1)} %g_hbm.1, f32[1,256,3584]{2,1,0:T(8,128)} %e_hbm.1, f32[32,3584]{1,0:T(8,128)} %bitcast.2), custom_call_target="tpu_custom_call" | custom-call | tf_op jit(solution)/shard_map/reduce/pallas_call | solution.py:281
  45.4 2.9 %finish.1 = (bf16[256,3584]{1,0:T(8,128)(2,1)}, f32[1,256,3584]{2,1,0:T(8,128)}, f32[32,3584]{1,0:T(8,128)}) custom-call(f32[4,256,896]{2,1,0:T(8,128)S(1)} %get-tuple-element.10.merged_ref, f32[4,32,896]{2,1,0:T(8,128)S(1)} %get-tuple-element.11.q_ref, bf16[32,192]{1,0:T(8,128)(2,1)S(1)} %get-tuple-element.12.inv_ref, ...), custom_call_target="tpu_custom_call" | custom-call | tf_op jit(solution)/shard_map/finish/pallas_call | solution.py:324

commit v3 on v2

--- a/solution.py
+++ b/solution.py
@@ -66,10 +66,10 @@
 
 
 def reduce_kernel(
-    g_hbm, e_hbm, qt_hbm, merged_out, q_out, inv_out, phat_out,
+    g_hbm, e_hbm, qt_hbm, merged_out, ag, left_out,
     g_v, e_v, qt_v, high_v, low_v, p_acc, p_loc, p_rs, p_ar, p_all,
-    x_src, x_buf, z_src, z_buf, ag,
-    load_sem, p_send, p_recv, x_send, x_recv, z_send, z_recv, ag_send, agz_recv, agx_recv,
+    x_src, x_buf, z_src, acc,
+    load_sem, p_send, p_recv, x_send, x_recv, z_send, z_recv, ag_send, agf_recv, agx_recv, ag_recv,
 ):
     dp, mp = lax.axis_index("dp"), lax.axis_index("mp")
     z, x = dp // NX, lax.rem(dp, NX)
@@ -109,20 +109,23 @@
             pltpu.make_async_copy(e_hbm.at[0, :, cols], e_v.at[i], load_sem.at[1, i]),
         )
 
-    @functools.partial(each, NX)
-    def _(i):
+    for i in range(NX):
         for copy in loads(i):
             copy.start()
-
-    barrier = pltpu.get_barrier_semaphore()
-
-    @functools.partial(each, n_dp - 1)
-    def _(i):
-        pl.semaphore_signal(barrier, inc=1, device_id=(dp_peer(i), mp), device_id_type=MESH)
-
-    @functools.partial(each, NMP - 1)
-    def _(i):
-        pl.semaphore_signal(barrier, inc=1, device_id=(dp, mp_peer(i)), device_id_type=MESH)
+        if i == 1:
+            barrier = pltpu.get_barrier_semaphore()
+
+            @functools.partial(each, n_dp - 1)
+            def _(i):
+                pl.semaphore_signal(
+                    barrier, inc=1, device_id=(dp_peer(i), mp), device_id_type=MESH
+                )
+
+            @functools.partial(each, NMP - 1)
+            def _(i):
+                pl.semaphore_signal(
+                    barrier, inc=1, device_id=(dp, mp_peer(i)), device_id_type=MESH
+                )
 
     drain = []
 
@@ -179,93 +182,110 @@
     )
 
     p_both = jnp.concatenate(split(p_t), axis=0)
-
-    @functools.partial(each, NX)
-    def _(i):
-        to = x_peer(i)
+    rows = RANK // NZ
+
+    def compute(to):
         both = jnp.dot(p_both, high_v[to], preferred_element_type=F32)
         both += jnp.dot(p_both, low_v[to], preferred_element_type=F32)
-        x_src[to] = both[:RANK] + both[RANK:]
+        block = both[:RANK] + both[RANK:]
+        for i in range(NZ):
+            x_src[to, lax.rem(i - z + NZ, NZ)] = block[i * rows : (i + 1) * rows]
+
+    @functools.partial(each, NX)
+    def _(i):
+        to = x_peer(i)
+        compute(to)
 
         @pl.when(i < NX - 1)
         def _():
-            send(x_src.at[to], x_buf.at[x], x_send, x_recv, z * NX + to, mp)
+            for f in (0, 2):
+                pair = x_src.at[to, pl.ds(2 + f + f // 2, 2)]
+                send(pair, x_buf.at[x, pl.ds(f, 2)], x_send, x_recv, z * NX + to, mp)
 
     drain.append((x_buf.at[pl.ds(0, NX - 1)], x_send))
-    x_buf[x] = x_src[x]
+
+    def direct(r, slot, n):
+        @functools.partial(each, n)
+        def _(i):
+            to = x_peer(i)
+            send(
+                x_src.at[to, r], acc.at[slot + x], z_send, z_recv, lax.rem(z + r, NZ) * NX + to, mp
+            )
+
+    for d in (1, 0, 2):
+        direct(1 + 3 * d, 4 + 4 * d, NX)
+    direct(0, 16, NX - 1)
+    acc[16 + x] = x_src[x, 0]
+    for f in (0, 2):
+        x_buf[x, f : f + 2] = x_src[x, 2 + f + f // 2 : 4 + f + f // 2]
 
     gram = lax.dot_general(
         p_t, p_t, (((1,), (1,)), ((), ())), precision=HIGHEST, preferred_element_type=F32
     )
     inverse = inverse_factor(gram)
-    inv_out[...] = stack_left(inverse)
-    phat_out[...] = stack_left(
-        jnp.dot(inverse, p_t, precision=HIGHEST, preferred_element_type=F32).T
-    )
+    left_out[ROWS:] = stack_left(inverse * (1.0 / n_dp))
 
     wait_bytes(x_buf.at[pl.ds(0, NX - 1)], x_recv)
-    block = jnp.sum(x_buf[...], axis=0)
-    rows = RANK // NZ
-    for i in range(NZ):
-        z_src[i] = block[i * rows : (i + 1) * rows]
-
-    @functools.partial(each, NZ - 1)
-    def _(i):
-        to = z_peer(i)
-        send(z_src.at[to], z_buf.at[z], z_send, z_recv, to * NX + x, mp)
-
-    drain.append((z_buf.at[pl.ds(0, NZ - 1)], z_send))
-    z_buf[z] = z_src[z]
-    wait_bytes(z_buf.at[pl.ds(0, NZ - 1)], z_recv)
-    ag[x, z] = jnp.sum(z_buf[...], axis=0)
-
-    @functools.partial(each, NZ - 1)
-    def _(i):
-        send(ag.at[x, z], ag.at[x, z], ag_send, agz_recv.at[z], z_peer(i) * NX + x, mp)
-
-    @functools.partial(each, NZ)
-    def _(i):
-        at = z_peer(NZ - 1 - i)
-
-        @pl.when(i > 0)
-        def _():
-            wait_bytes(ag.at[x, at], agz_recv.at[at])
-
-        @functools.partial(each, NX - 1)
-        def _(j):
-            send(ag.at[x, at], ag.at[x, at], ag_send, agx_recv, z * NX + x_peer(j), mp)
-
-    drain.append((ag.at[pl.ds(0, NX - 1)], ag_send))
-    drain.append((ag.at[0, pl.ds(0, NZ - 1)], ag_send))
-    wait_bytes(ag.at[pl.ds(0, NX - 1)], agx_recv)
-    for i in range(NX):
-        q_out[i] = jnp.concatenate([ag[i, j] for j in range(NZ)], axis=0)
+    for f in (1, 2, 0, 3):
+        z_src[f] = jnp.sum(x_buf[:, f], axis=0)
+        to = lax.rem(z + 2 + f + f // 2, NZ)
+        send(z_src.at[f], acc.at[f], z_send, z_recv, to * NX + x, mp)
+
+    drain.append((acc.at[pl.ds(0, 19)], z_send))
+    p_hat = jnp.dot(inverse, p_t, precision=HIGHEST, preferred_element_type=F32).T
+    onto = jnp.dot(p_hat, inverse, precision=HIGHEST, preferred_element_type=F32)
+    left_out[:ROWS] = stack_left(onto * (1.0 / n_dp))
+    wait_bytes(acc.at[pl.ds(0, 19)], z_recv)
+    own = x * NZ + z
+    ag[own] = jnp.sum(acc[...], axis=0)
+
+    def spread(piece, r, j, sem):
+        to = lax.rem(z + r, NZ) * NX + lax.rem(x + j, NX)
+        send(ag.at[piece], ag.at[piece], ag_send, sem, to, mp)
+
+    for j in (2, 1, 3):
+        spread(own, 0, j, agx_recv.at[j])
+    for f, r in enumerate((3, 5)):
+        spread(own, r, 0, agf_recv.at[f])
+    for j in (0, 2, 1, 3):
+        spread(own, 4, j, ag_recv)
+    for r in (2, 6, 1, 7):
+        spread(own, r, 0, ag_recv)
+    for j in (1, 3, 2):
+        piece = lax.rem(x + NX - j, NX) * NZ + z
+        wait_bytes(ag.at[piece], agx_recv.at[j])
+        for r in (2, 6, 1, 7):
+            spread(piece, r, 0, ag_recv)
+    for f, r in enumerate((3, 5)):
+        piece = x * NZ + lax.rem(z + NZ - r, NZ)
+        wait_bytes(ag.at[piece], agf_recv.at[f])
+        for j in (2, 1, 3):
+            spread(piece, 0, j, ag_recv)
+
+    drain.append((ag.at[pl.ds(0, n_dp - 1)], ag_send))
+    wait_bytes(ag.at[pl.ds(0, n_dp - 6)], ag_recv)
 
     for ref, sem in drain:
         wait_bytes(ref, sem)
 
 
-def finish_kernel(
-    replicas, merged_ref, q_ref, inv_ref, phat_ref, u_hbm, n_hbm, q_hbm, u_v, n_v, q_v, sems
-):
+def finish_kernel(merged_ref, q_ref, left_ref, u_hbm, n_hbm, q_hbm, u_v, n_v, q_v, sems):
     blocks, _, width = merged_ref.shape
     half = ROWS // 2
 
     def block(i, carry):
         cols = pl.ds(pl.multiple_of(i * width, 128), width)
-        q_next = jnp.dot(inv_ref[...], stack_right(q_ref[i]), preferred_element_type=F32)
-        q_next = q_next * (1.0 / replicas)
-        q_v[i] = q_next
-        pltpu.make_async_copy(q_v.at[i], q_hbm.at[:, cols], sems.at[0]).start()
-        right = stack_right(q_next)
+        right = stack_right(jnp.concatenate([q_ref[i * NZ + j] for j in range(NZ)], axis=0))
         for h in range(2):
             rows = slice(h * half, (h + 1) * half)
             at = pl.ds(h * half, half)
-            recon = jnp.dot(phat_ref[rows], right, preferred_element_type=F32)
+            recon = jnp.dot(left_ref[rows], right, preferred_element_type=F32)
             n_v[i, rows] = merged_ref[i, rows] - recon
             pltpu.make_async_copy(n_v.at[i, at], n_hbm.at[0, at, cols], sems.at[1]).start()
             u_v[i, rows] = recon.astype(BF16)
             pltpu.make_async_copy(u_v.at[i, at], u_hbm.at[at, cols], sems.at[2]).start()
+        q_v[i] = jnp.dot(left_ref[ROWS:], right, preferred_element_type=F32)
+        pltpu.make_async_copy(q_v.at[i], q_hbm.at[:, cols], sems.at[0]).start()
         return carry
 
     lax.fori_loop(0, blocks, block, 0)
@@ -282,12 +302,11 @@
         reduce_kernel,
         out_shape=(
             jax.ShapeDtypeStruct((NX, ROWS, width), F32),
-            jax.ShapeDtypeStruct((NX, RANK, width), F32),
-            jax.ShapeDtypeStruct((RANK, 6 * RANK), BF16),
-            jax.ShapeDtypeStruct((ROWS, 6 * RANK), BF16),
+            jax.ShapeDtypeStruct((NX * NZ, piece, width), F32),
+            jax.ShapeDtypeStruct((ROWS + RANK, 6 * RANK), BF16),
         ),
         in_specs=[HBM] * 3,
-        out_specs=[VMEM] * 4,
+        out_specs=[VMEM] * 3,
         scratch_shapes=[
             pltpu.VMEM((NX, ROWS, width), BF16),
             pltpu.VMEM((NX, ROWS, width), F32),
@@ -299,11 +318,10 @@
             pltpu.VMEM((NMP, 8, 128), F32),
             pltpu.VMEM((NZ * NX, 8, 128), F32),
             pltpu.VMEM((NMP, 8, 128), F32),
-            pltpu.VMEM((NX, RANK, width), F32),
-            pltpu.VMEM((NX, RANK, width), F32),
-            pltpu.VMEM((NZ, piece, width), F32),
-            pltpu.VMEM((NZ, piece, width), F32),
             pltpu.VMEM((NX, NZ, piece, width), F32),
+            pltpu.VMEM((NX, 4, piece, width), F32),
+            pltpu.VMEM((4, piece, width), F32),
+            pltpu.VMEM((20, piece, width), F32),
             dma((3, NX)),
             dma((3,)),
             dma((3,)),
@@ -312,7 +330,8 @@
             dma,
             dma,
             dma,
-            dma((NZ,)),
+            dma((2,)),
+            dma((NX,)),
             dma,
         ],
         compiler_params=pltpu.CompilerParams(
@@ -322,13 +341,13 @@
     )(*(pltpu.with_memory_space_constraint(a, pltpu.HBM) for a in (grads, errors, q_init.T)))
 
     update, new_errors, q_next = pl.pallas_call(
-        functools.partial(finish_kernel, lax.axis_size("dp")),
+        finish_kernel,
         out_shape=(
             jax.ShapeDtypeStruct((ROWS, columns), BF16),
             jax.ShapeDtypeStruct((1, ROWS, columns), F32),
             jax.ShapeDtypeStruct((RANK, columns), F32),
         ),
-        in_specs=[VMEM] * 4,
+        in_specs=[VMEM] * 3,
         out_specs=[HBM] * 3,
         scratch_shapes=[
             pltpu.VMEM((NX, ROWS, width), BF16),

time: 48.8 us -> 47.9 us (0.982)
  Pallas kernels: 47.7 us -> 46.3 us
    pallas_call x1, Pallas kernels: 44.8 us -> 43.5 us  [body(): pl.pallas_call(reduce_kernel, out_shape=(jax.ShapeDtypeStruct((NX, ROWS,...]
where the time goes in v3:
time: 47.9 us; the launch traced here: 47 us
  Pallas kernels  46.3 us (97%)
  between operations  0.64 us (1%)
    pallas_call x1, Pallas kernels, body(): pl.pallas_call(reduce_kernel, out_shape=(jax.ShapeDtypeStruct((NX, ROWS,...  43.5 us
    pallas_call x1, Pallas kernels, body(): pl.pallas_call(finish_kernel, out_shape=(jax.ShapeDtypeStruct((ROWS, colu...  2.79 us

profile of v3, /device:TPU:8, one launch (start us, length us, event | category | flops | bytes accessed | tf_op | source)
XLA Modules:
  0.0 47.0 jit_solution(8703184109577006809)
XLA Ops:
  0.6 43.5 %reduce.1 = (f32[4,256,896]{2,1,0:T(8,128)S(1)}, f32[32,4,896]{2,1,0:T(4,128)S(1)}, bf16[288,192]{1,0:T(8,128)(2,1)S(1)}) custom-call(bf16[1,256,3584]{2,1,0:T(8,128)(2,1)} %g_hbm.1, f32[1,256,3584]{2,1,0:T(8,128)} %e_hbm.1, f32[32,3584]{1,0:T(8,128)} %bitcast.2), custom_call_target="tpu_custom_call" | custom-call | tf_op jit(solution)/shard_map/reduce/pallas_call | solution.py:301
  44.2 2.8 %finish.1 = (bf16[256,3584]{1,0:T(8,128)(2,1)}, f32[1,256,3584]{2,1,0:T(8,128)}, f32[32,3584]{1,0:T(8,128)}) custom-call(f32[4,256,896]{2,1,0:T(8,128)S(1)} %get-tuple-element.9.merged_ref, f32[32,4,896]{2,1,0:T(4,128)S(1)} %get-tuple-element.10.q_ref, bf16[288,192]{1,0:T(8,128)(2,1)S(1)} %get-tuple-element.11.left_ref), custom_call_target="tpu_custom_call" | custom-call | tf_op jit(solution)/shard_map/finish/pallas_call | solution.py:343

commit v4 on v3

--- a/solution.py
+++ b/solution.py
@@ -86,8 +86,8 @@
     def dp_peer(i):
         return z_peer(i // NX) * NX + x_peer(lax.rem(i, NX))
 
-    def mp_peer(i):
-        return lax.rem(y + around(i // 2, NMP // 2), NMP // 2) * 2 + lax.rem(core + i + 1, 2)
+    def y_peer(i):
+        return lax.rem(y + around(i, NMP // 2), NMP // 2)
 
     def each(n, act):
         lax.fori_loop(0, n, lambda i, c: (act(i), c)[1], 0)
@@ -115,17 +115,33 @@
         if i == 1:
             barrier = pltpu.get_barrier_semaphore()
 
-            @functools.partial(each, n_dp - 1)
-            def _(i):
-                pl.semaphore_signal(
-                    barrier, inc=1, device_id=(dp_peer(i), mp), device_id_type=MESH
-                )
-
-            @functools.partial(each, NMP - 1)
-            def _(i):
-                pl.semaphore_signal(
-                    barrier, inc=1, device_id=(dp, mp_peer(i)), device_id_type=MESH
-                )
+            @pl.when(core == 1)
+            def _():
+                @functools.partial(each, n_dp - 1)
+                def _(i):
+                    pl.semaphore_signal(
+                        barrier, inc=1, device_id=(dp_peer(i), mp), device_id_type=MESH
+                    )
+
+                @functools.partial(each, NMP // 2)
+                def _(i):
+                    pl.semaphore_signal(
+                        barrier, inc=1, device_id=(dp, y_peer(i) * 2), device_id_type=MESH
+                    )
+
+                @functools.partial(each, NMP // 2 - 1)
+                def _(i):
+                    pl.semaphore_signal(
+                        barrier, inc=1, device_id=(dp, y_peer(i) * 2 + 1), device_id_type=MESH
+                    )
+
+            @pl.when(core == 0)
+            def _():
+                @functools.partial(each, NMP // 2)
+                def _(i):
+                    pl.semaphore_signal(
+                        barrier, inc=1, device_id=(dp, y_peer(i) * 2 + 1), device_id_type=MESH
+                    )
 
     drain = []
 
@@ -144,39 +160,52 @@
         p_acc[...] += dot_t(high, q_both) + dot_t(low, q_both)
 
     p_t = (p_acc[:, :RANK] + p_acc[:, RANK:]).T
-    for t in range(NMP):
-        p_loc[t] = p_t[8 * (t % 4) : 8 * (t % 4) + 8, 128 * (t // 4) : 128 * (t // 4) + 128]
-
-    pl.semaphore_wait(barrier, n_dp - 1 + NMP - 1)
-
-    @functools.partial(each, NMP - 1)
-    def _(i):
-        to = mp_peer(i)
-        send(p_loc.at[to], p_rs.at[mp], p_send.at[0], p_recv.at[0], dp, to)
-
-    drain.append((p_rs.at[pl.ds(0, NMP - 1)], p_send.at[0]))
-    p_rs[mp] = p_loc[mp]
-    wait_bytes(p_rs.at[pl.ds(0, NMP - 1)], p_recv.at[0])
-    p_ar[dp] = jnp.sum(p_rs[...], axis=0)
-
-    @functools.partial(each, n_dp - 1)
-    def _(i):
-        send(p_ar.at[dp], p_ar.at[dp], p_send.at[1], p_recv.at[1], dp_peer(i), mp)
-
-    drain.append((p_ar.at[pl.ds(0, n_dp - 1)], p_send.at[1]))
-    wait_bytes(p_ar.at[pl.ds(0, n_dp - 1)], p_recv.at[1])
-    p_all[mp] = jnp.sum(p_ar[...], axis=0)
-
-    @functools.partial(each, NMP - 1)
-    def _(i):
-        send(p_all.at[mp], p_all.at[mp], p_send.at[2], p_recv.at[2], dp, mp_peer(i))
-
-    drain.append((p_all.at[pl.ds(0, NMP - 1)], p_send.at[2]))
-    wait_bytes(p_all.at[pl.ds(0, NMP - 1)], p_recv.at[2])
+    for t in range(NMP // 2):
+        p_loc[t] = p_t[16 * (t % 2) : 16 * (t % 2) + 16, 128 * (t // 2) : 128 * (t // 2) + 128]
+
+    @pl.when(core == 1)
+    def _():
+        pl.semaphore_wait(barrier, n_dp - 1 + NMP - 1)
+
+    @pl.when(core == 0)
+    def _():
+        pl.semaphore_wait(barrier, NMP // 2)
+
+    ys = NMP // 2
+
+    def scatter(i):
+        to = y_peer(i)
+        send(p_loc.at[to], p_rs.at[mp], p_send.at[0], p_recv.at[0], dp, to * 2 + 1)
+
+    def gather(i, c):
+        send(p_all.at[y], p_all.at[y], p_send.at[2], p_recv.at[2], dp, y_peer(i) * 2 + c)
+
+    @pl.when(core == 0)
+    def _():
+        each(ys, scatter)
+        wait_bytes(p_all.at[pl.ds(0, ys)], p_recv.at[2])
+
+    @pl.when(core == 1)
+    def _():
+        each(ys - 1, scatter)
+        p_rs[mp] = p_loc[y]
+        wait_bytes(p_rs.at[pl.ds(0, NMP - 1)], p_recv.at[0])
+        p_ar[dp] = jnp.sum(p_rs[...], axis=0)
+
+        @functools.partial(each, n_dp - 1)
+        def _(i):
+            send(p_ar.at[dp], p_ar.at[dp], p_send.at[1], p_recv.at[1], dp_peer(i), mp)
+
+        wait_bytes(p_ar.at[pl.ds(0, n_dp - 1)], p_recv.at[1])
+        p_all[y] = jnp.sum(p_ar[...], axis=0)
+        each(ys, lambda i: gather(i, 0))
+        each(ys - 1, lambda i: gather(i, 1))
+        wait_bytes(p_all.at[pl.ds(0, ys - 1)], p_recv.at[2])
+
     p_t = jnp.concatenate(
         [
-            jnp.concatenate([p_all[t] for t in range(4)], axis=0),
-            jnp.concatenate([p_all[t] for t in range(4, 8)], axis=0),
+            jnp.concatenate([p_all[0], p_all[1]], axis=0),
+            jnp.concatenate([p_all[2], p_all[3]], axis=0),
         ],
         axis=1,
     )
@@ -267,6 +296,16 @@
 
     for ref, sem in drain:
         wait_bytes(ref, sem)
+
+    @pl.when(core == 0)
+    def _():
+        wait_bytes(p_rs.at[pl.ds(0, ys)], p_send.at[0])
+
+    @pl.when(core == 1)
+    def _():
+        wait_bytes(p_rs.at[pl.ds(0, ys - 1)], p_send.at[0])
+        wait_bytes(p_ar.at[pl.ds(0, n_dp - 1)], p_send.at[1])
+        wait_bytes(p_rs.at[pl.ds(0, NMP - 1)], p_send.at[2])
 
 
 def finish_kernel(merged_ref, q_ref, left_ref, u_hbm, n_hbm, q_hbm, u_v, n_v, q_v, sems):
@@ -314,10 +353,10 @@
             pltpu.VMEM((NX, ROWS, width), BF16),
             pltpu.VMEM((NX, ROWS, width), BF16),
             pltpu.VMEM((ROWS, 2 * RANK), F32),
-            pltpu.VMEM((NMP, 8, 128), F32),
-            pltpu.VMEM((NMP, 8, 128), F32),
-            pltpu.VMEM((NZ * NX, 8, 128), F32),
-            pltpu.VMEM((NMP, 8, 128), F32),
+            pltpu.VMEM((NMP // 2, 16, 128), F32),
+            pltpu.VMEM((NMP, 16, 128), F32),
+            pltpu.VMEM((NZ * NX, 16, 128), F32),
+            pltpu.VMEM((NMP // 2, 16, 128), F32),
             pltpu.VMEM((NX, NZ, piece, width), F32),
             pltpu.VMEM((NX, 4, piece, width), F32),
             pltpu.VMEM((4, piece, width), F32),

time: 47.9 us -> 46.8 us (0.977)
  Pallas kernels: 46.3 us -> 45.7 us
    pallas_call x1, Pallas kernels: 43.5 us -> 42.9 us  [body(): pl.pallas_call(reduce_kernel, out_shape=(jax.ShapeDtypeStruct((NX, ROWS,...]
where the time goes in v4:
time: 46.8 us; the launch traced here: 46.3 us
  Pallas kernels  45.7 us (98%)
  between operations  0.64 us (1%)
    pallas_call x1, Pallas kernels, body(): pl.pallas_call(reduce_kernel, out_shape=(jax.ShapeDtypeStruct((NX, ROWS,...  42.9 us
    pallas_call x1, Pallas kernels, body(): pl.pallas_call(finish_kernel, out_shape=(jax.ShapeDtypeStruct((ROWS, colu...  2.79 us

profile of v4, /device:TPU:8, one launch (start us, length us, event | category | flops | bytes accessed | tf_op | source)
XLA Modules:
  0.0 46.3 jit_solution(3553515773728926560)
XLA Ops:
  0.6 42.9 %reduce.1 = (f32[4,256,896]{2,1,0:T(8,128)S(1)}, f32[32,4,896]{2,1,0:T(4,128)S(1)}, bf16[288,192]{1,0:T(8,128)(2,1)S(1)}) custom-call(bf16[1,256,3584]{2,1,0:T(8,128)(2,1)} %g_hbm.1, f32[1,256,3584]{2,1,0:T(8,128)} %e_hbm.1, f32[32,3584]{1,0:T(8,128)} %bitcast.2), custom_call_target="tpu_custom_call" | custom-call | tf_op jit(solution)/shard_map/reduce/pallas_call | solution.py:340
  43.5 2.8 %finish.1 = (bf16[256,3584]{1,0:T(8,128)(2,1)}, f32[1,256,3584]{2,1,0:T(8,128)}, f32[32,3584]{1,0:T(8,128)}) custom-call(f32[4,256,896]{2,1,0:T(8,128)S(1)} %get-tuple-element.9.merged_ref, f32[32,4,896]{2,1,0:T(4,128)S(1)} %get-tuple-element.10.q_ref, bf16[288,192]{1,0:T(8,128)(2,1)S(1)} %get-tuple-element.11.left_ref), custom_call_target="tpu_custom_call" | custom-call | tf_op jit(solution)/shard_map/finish/pallas_call | solution.py:382

commit v5 on v4

--- a/solution.py
+++ b/solution.py
@@ -68,8 +68,8 @@
 def reduce_kernel(
     g_hbm, e_hbm, qt_hbm, merged_out, ag, left_out,
     g_v, e_v, qt_v, high_v, low_v, p_acc, p_loc, p_rs, p_ar, p_all,
-    x_src, x_buf, z_src, acc,
-    load_sem, p_send, p_recv, x_send, x_recv, z_send, z_recv, ag_send, agf_recv, agx_recv, ag_recv,
+    x_src, x_buf, z_src, acc, aux, inv_v,
+    load_sem, p_send, p_recv, x_send, x_recv, z_send, z_recv, ag_send, agf_recv, agx_recv, ag_recv, aux_recv, inv_sem,
 ):
     dp, mp = lax.axis_index("dp"), lax.axis_index("mp")
     z, x = dp // NX, lax.rem(dp, NX)
@@ -248,11 +248,18 @@
     for f in (0, 2):
         x_buf[x, f : f + 2] = x_src[x, 2 + f + f // 2 : 4 + f + f // 2]
 
-    gram = lax.dot_general(
-        p_t, p_t, (((1,), (1,)), ((), ())), precision=HIGHEST, preferred_element_type=F32
-    )
-    inverse = inverse_factor(gram)
-    left_out[ROWS:] = stack_left(inverse * (1.0 / n_dp))
+    def factor():
+        gram = lax.dot_general(
+            p_t, p_t, (((1,), (1,)), ((), ())), precision=HIGHEST, preferred_element_type=F32
+        )
+        inverse = inverse_factor(gram)
+        return inverse
+
+    def project(inverse):
+        left_out[ROWS:] = stack_left(inverse * (1.0 / n_dp))
+        p_hat = jnp.dot(inverse, p_t, precision=HIGHEST, preferred_element_type=F32).T
+        onto = jnp.dot(p_hat, inverse, precision=HIGHEST, preferred_element_type=F32)
+        left_out[:ROWS] = stack_left(onto * (1.0 / n_dp))
 
     wait_bytes(x_buf.at[pl.ds(0, NX - 1)], x_recv)
     for f in (1, 2, 0, 3):
@@ -261,38 +268,71 @@
         send(z_src.at[f], acc.at[f], z_send, z_recv, to * NX + x, mp)
 
     drain.append((acc.at[pl.ds(0, 19)], z_send))
-    p_hat = jnp.dot(inverse, p_t, precision=HIGHEST, preferred_element_type=F32).T
-    onto = jnp.dot(p_hat, inverse, precision=HIGHEST, preferred_element_type=F32)
-    left_out[:ROWS] = stack_left(onto * (1.0 / n_dp))
     wait_bytes(acc.at[pl.ds(0, 19)], z_recv)
     own = x * NZ + z
     ag[own] = jnp.sum(acc[...], axis=0)
 
-    def spread(piece, r, j, sem):
+    near, far = (2, 6, 1, 7), (3, 5)
+
+    def spread(src, piece, r, j, c, sem):
         to = lax.rem(z + r, NZ) * NX + lax.rem(x + j, NX)
-        send(ag.at[piece], ag.at[piece], ag_send, sem, to, mp)
-
-    for j in (2, 1, 3):
-        spread(own, 0, j, agx_recv.at[j])
-    for f, r in enumerate((3, 5)):
-        spread(own, r, 0, agf_recv.at[f])
-    for j in (0, 2, 1, 3):
-        spread(own, 4, j, ag_recv)
-    for r in (2, 6, 1, 7):
-        spread(own, r, 0, ag_recv)
-    for j in (1, 3, 2):
-        piece = lax.rem(x + NX - j, NX) * NZ + z
-        wait_bytes(ag.at[piece], agx_recv.at[j])
-        for r in (2, 6, 1, 7):
-            spread(piece, r, 0, ag_recv)
-    for f, r in enumerate((3, 5)):
-        piece = x * NZ + lax.rem(z + NZ - r, NZ)
-        wait_bytes(ag.at[piece], agf_recv.at[f])
+        send(src, ag.at[piece], ag_send, sem, to, y * 2 + c)
+
+    @pl.when(core == 0)
+    def _():
         for j in (2, 1, 3):
-            spread(piece, 0, j, ag_recv)
-
-    drain.append((ag.at[pl.ds(0, n_dp - 1)], ag_send))
-    wait_bytes(ag.at[pl.ds(0, n_dp - 6)], ag_recv)
+            to = z * NX + lax.rem(x + j, NX)
+            send(ag.at[own], aux.at[j - 1], ag_send, aux_recv.at[j - 1], to, mp + 1)
+        for f, r in enumerate(far):
+            to = lax.rem(z + r, NZ) * NX + x
+            send(ag.at[own], aux.at[3 + f], ag_send, aux_recv.at[3 + f], to, mp + 1)
+        for j in (0, 2, 1, 3):
+            spread(ag.at[own], own, 4, j, 0, ag_recv)
+        for r in near:
+            spread(ag.at[own], own, r, 0, 0, ag_recv)
+        inverse = factor()
+        inv_v[...] = jnp.concatenate([inverse, jnp.zeros((RANK, 3 * RANK), F32)], axis=1)
+        send(inv_v, inv_v, inv_sem.at[0], inv_sem.at[1], dp, mp + 1)
+        project(inverse)
+        wait_bytes(ag.at[pl.ds(0, n_dp - 1)], ag_recv)
+        wait_bytes(ag.at[pl.ds(0, 13)], ag_send)
+        wait_bytes(inv_v, inv_sem.at[0])
+
+    @pl.when(core == 1)
+    def _():
+        for j in (2, 1, 3):
+            spread(ag.at[own], own, 0, j, 1, agx_recv.at[j])
+        for f, r in enumerate(far):
+            spread(ag.at[own], own, r, 0, 1, agf_recv.at[f])
+        for j in (0, 2, 1, 3):
+            spread(ag.at[own], own, 4, j, 1, ag_recv)
+        for r in near:
+            spread(ag.at[own], own, r, 0, 1, ag_recv)
+        for j in (1, 3, 2):
+            piece = lax.rem(x + NX - j, NX) * NZ + z
+            wait_bytes(ag.at[piece], agx_recv.at[j])
+            for r in near:
+                spread(ag.at[piece], piece, r, 0, 1, ag_recv)
+        for f, r in enumerate(far):
+            piece = x * NZ + lax.rem(z + NZ - r, NZ)
+            wait_bytes(ag.at[piece], agf_recv.at[f])
+            for j in (2, 1, 3):
+                spread(ag.at[piece], piece, 0, j, 1, ag_recv)
+        for j in (1, 3, 2):
+            piece = lax.rem(x + NX - j, NX) * NZ + z
+            wait_bytes(aux.at[j - 1], aux_recv.at[j - 1])
+            for r in near + (0,):
+                spread(aux.at[j - 1], piece, r, 0, 0, ag_recv)
+        for f, r in enumerate(far):
+            piece = x * NZ + lax.rem(z + NZ - r, NZ)
+            wait_bytes(aux.at[3 + f], aux_recv.at[3 + f])
+            for j in (2, 1, 3, 0):
+                spread(aux.at[3 + f], piece, 0, j, 0, ag_recv)
+        wait_bytes(inv_v, inv_sem.at[1])
+        project(inv_v[:, :RANK])
+        wait_bytes(ag.at[pl.ds(0, n_dp - 6)], ag_recv)
+        wait_bytes(ag.at[pl.ds(0, n_dp - 1)], ag_send)
+        wait_bytes(ag.at[pl.ds(0, 23)], ag_send)
 
     for ref, sem in drain:
         wait_bytes(ref, sem)
@@ -361,6 +401,8 @@
             pltpu.VMEM((NX, 4, piece, width), F32),
             pltpu.VMEM((4, piece, width), F32),
             pltpu.VMEM((20, piece, width), F32),
+            pltpu.VMEM((5, piece, width), F32),
+            pltpu.VMEM((RANK, 4 * RANK), F32),
             dma((3, NX)),
             dma((3,)),
             dma((3,)),
@@ -372,6 +414,8 @@
             dma((2,)),
             dma((NX,)),
             dma,
+            dma((5,)),
+            dma((2,)),
         ],
         compiler_params=pltpu.CompilerParams(
             collective_id=0, has_side_effects=True, vmem_limit_bytes=40 << 20

time: 46.8 us -> 45.8 us (0.979)
  Pallas kernels: 45.7 us -> 44.7 us
    pallas_call x1, Pallas kernels: 42.9 us -> 41.9 us  [body(): pl.pallas_call(reduce_kernel, out_shape=(jax.ShapeDtypeStruct((NX, ROWS,...]
where the time goes in v5:
time: 45.8 us; the launch traced here: 45.3 us
  Pallas kernels  44.7 us (98%)
  between operations  0.64 us (1%)
    pallas_call x1, Pallas kernels, body(): pl.pallas_call(reduce_kernel, out_shape=(jax.ShapeDtypeStruct((NX, ROWS,...  41.9 us
    pallas_call x1, Pallas kernels, body(): pl.pallas_call(finish_kernel, out_shape=(jax.ShapeDtypeStruct((ROWS, colu...  2.79 us

profile of v5, /device:TPU:8, one launch (start us, length us, event | category | flops | bytes accessed | tf_op | source)
XLA Modules:
  0.0 45.3 jit_solution(16696896181707449130)
XLA Ops:
  0.6 41.9 %reduce.1 = (f32[4,256,896]{2,1,0:T(8,128)S(1)}, f32[32,4,896]{2,1,0:T(4,128)S(1)}, bf16[288,192]{1,0:T(8,128)(2,1)S(1)}) custom-call(bf16[1,256,3584]{2,1,0:T(8,128)(2,1)} %g_hbm.1, f32[1,256,3584]{2,1,0:T(8,128)} %e_hbm.1, f32[32,3584]{1,0:T(8,128)} %bitcast.2), custom_call_target="tpu_custom_call" | custom-call | tf_op jit(solution)/shard_map/reduce/pallas_call | solution.py:380
  42.5 2.8 %finish.1 = (bf16[256,3584]{1,0:T(8,128)(2,1)}, f32[1,256,3584]{2,1,0:T(8,128)}, f32[32,3584]{1,0:T(8,128)}) custom-call(f32[4,256,896]{2,1,0:T(8,128)S(1)} %get-tuple-element.9.merged_ref, f32[32,4,896]{2,1,0:T(4,128)S(1)} %get-tuple-element.10.q_ref, bf16[288,192]{1,0:T(8,128)(2,1)S(1)} %get-tuple-element.11.left_ref), custom_call_target="tpu_custom_call" | custom-call | tf_op jit(solution)/shard_map/finish/pallas_call | solution.py:426

commit v6 on v5

--- a/solution.py
+++ b/solution.py
@@ -68,8 +68,8 @@
 def reduce_kernel(
     g_hbm, e_hbm, qt_hbm, merged_out, ag, left_out,
     g_v, e_v, qt_v, high_v, low_v, p_acc, p_loc, p_rs, p_ar, p_all,
-    x_src, x_buf, z_src, acc, aux, inv_v,
-    load_sem, p_send, p_recv, x_send, x_recv, z_send, z_recv, ag_send, agf_recv, agx_recv, ag_recv, aux_recv, inv_sem,
+    x_src, x_buf, y_buf, z_src, acc, aux, inv_v,
+    load_sem, p_send, p_recv, x_send, x_recv, z_send, z_recv, ag_send, agf_recv, agx_recv, ag_recv, aux_recv, inv_sem, y_recv,
 ):
     dp, mp = lax.axis_index("dp"), lax.axis_index("mp")
     z, x = dp // NX, lax.rem(dp, NX)
@@ -143,7 +143,6 @@
                         barrier, inc=1, device_id=(dp, y_peer(i) * 2 + 1), device_id_type=MESH
                     )
 
-    drain = []
 
     p_acc[...] = jnp.zeros_like(p_acc)
 
@@ -225,13 +224,18 @@
         to = x_peer(i)
         compute(to)
 
-        @pl.when(i < NX - 1)
-        def _():
+        def pairs(buf, sem):
             for f in (0, 2):
                 pair = x_src.at[to, pl.ds(2 + f + f // 2, 2)]
-                send(pair, x_buf.at[x, pl.ds(f, 2)], x_send, x_recv, z * NX + to, mp)
-
-    drain.append((x_buf.at[pl.ds(0, NX - 1)], x_send))
+                send(pair, buf.at[x, pl.ds(f, 2)], x_send, sem, z * NX + to, y * 2 + 1)
+
+        @pl.when(core == 0)
+        def _():
+            pairs(y_buf, y_recv)
+
+        @pl.when(jnp.logical_and(core == 1, i < NX - 1))
+        def _():
+            pairs(x_buf, x_recv)
 
     def direct(r, slot, n):
         @functools.partial(each, n)
@@ -245,8 +249,6 @@
         direct(1 + 3 * d, 4 + 4 * d, NX)
     direct(0, 16, NX - 1)
     acc[16 + x] = x_src[x, 0]
-    for f in (0, 2):
-        x_buf[x, f : f + 2] = x_src[x, 2 + f + f // 2 : 4 + f + f // 2]
 
     def factor():
         gram = lax.dot_general(
@@ -261,13 +263,21 @@
         onto = jnp.dot(p_hat, inverse, precision=HIGHEST, preferred_element_type=F32)
         left_out[:ROWS] = stack_left(onto * (1.0 / n_dp))
 
-    wait_bytes(x_buf.at[pl.ds(0, NX - 1)], x_recv)
-    for f in (1, 2, 0, 3):
-        z_src[f] = jnp.sum(x_buf[:, f], axis=0)
-        to = lax.rem(z + 2 + f + f // 2, NZ)
-        send(z_src.at[f], acc.at[f], z_send, z_recv, to * NX + x, mp)
-
-    drain.append((acc.at[pl.ds(0, 19)], z_send))
+    def pass_on(buf, c):
+        for f in (1, 2, 0, 3):
+            z_src[c, f] = jnp.sum(buf[:, f], axis=0)
+            to = lax.rem(z + 2 + f + f // 2, NZ)
+            send(z_src.at[c, f], acc.at[f], z_send, z_recv, to * NX + x, y * 2 + c)
+
+    @pl.when(core == 1)
+    def _():
+        for f in (0, 2):
+            x_buf[x, f : f + 2] = x_src[x, 2 + f + f // 2 : 4 + f + f // 2]
+        wait_bytes(x_buf.at[pl.ds(0, NX - 1)], x_recv)
+        pass_on(x_buf, 1)
+        wait_bytes(y_buf, y_recv)
+        pass_on(y_buf, 0)
+
     wait_bytes(acc.at[pl.ds(0, 19)], z_recv)
     own = x * NZ + z
     ag[own] = jnp.sum(acc[...], axis=0)
@@ -334,16 +344,17 @@
         wait_bytes(ag.at[pl.ds(0, n_dp - 1)], ag_send)
         wait_bytes(ag.at[pl.ds(0, 23)], ag_send)
 
-    for ref, sem in drain:
-        wait_bytes(ref, sem)
-
     @pl.when(core == 0)
     def _():
         wait_bytes(p_rs.at[pl.ds(0, ys)], p_send.at[0])
+        wait_bytes(x_buf, x_send)
+        wait_bytes(acc.at[pl.ds(0, 15)], z_send)
 
     @pl.when(core == 1)
     def _():
         wait_bytes(p_rs.at[pl.ds(0, ys - 1)], p_send.at[0])
+        wait_bytes(x_buf.at[pl.ds(0, NX - 1)], x_send)
+        wait_bytes(ag.at[pl.ds(0, 23)], z_send)
         wait_bytes(p_ar.at[pl.ds(0, n_dp - 1)], p_send.at[1])
         wait_bytes(p_rs.at[pl.ds(0, NMP - 1)], p_send.at[2])
 
@@ -399,7 +410,8 @@
             pltpu.VMEM((NMP // 2, 16, 128), F32),
             pltpu.VMEM((NX, NZ, piece, width), F32),
             pltpu.VMEM((NX, 4, piece, width), F32),
-            pltpu.VMEM((4, piece, width), F32),
+            pltpu.VMEM((NX, 4, piece, width), F32),
+            pltpu.VMEM((2, 4, piece, width), F32),
             pltpu.VMEM((20, piece, width), F32),
             pltpu.VMEM((5, piece, width), F32),
             pltpu.VMEM((RANK, 4 * RANK), F32),
@@ -416,6 +428,7 @@
             dma,
             dma((5,)),
             dma((2,)),
+            dma,
         ],
         compiler_params=pltpu.CompilerParams(
             collective_id=0, has_side_effects=True, vmem_limit_bytes=40 << 20

time: 45.8 us -> 45.1 us (0.985)
  Pallas kernels: 44.7 us -> 43.9 us
    pallas_call x1, Pallas kernels: 41.9 us -> 41.1 us  [body(): pl.pallas_call(reduce_kernel, out_shape=(jax.ShapeDtypeStruct((NX, ROWS,...]
where the time goes in v6:
time: 45.1 us; the launch traced here: 44.5 us
  Pallas kernels  43.9 us (97%)
  between operations  0.64 us (1%)
    pallas_call x1, Pallas kernels, body(): pl.pallas_call(reduce_kernel, out_shape=(jax.ShapeDtypeStruct((NX, ROWS,...  41.1 us
    pallas_call x1, Pallas kernels, body(): pl.pallas_call(finish_kernel, out_shape=(jax.ShapeDtypeStruct((ROWS, colu...  2.79 us

profile of v6, /device:TPU:8, one launch (start us, length us, event | category | flops | bytes accessed | tf_op | source)
XLA Modules:
  0.0 44.5 jit_solution(12914194408803543828)
XLA Ops:
  0.6 41.1 %reduce.1 = (f32[4,256,896]{2,1,0:T(8,128)S(1)}, f32[32,4,896]{2,1,0:T(4,128)S(1)}, bf16[288,192]{1,0:T(8,128)(2,1)S(1)}) custom-call(bf16[1,256,3584]{2,1,0:T(8,128)(2,1)} %g_hbm.1, f32[1,256,3584]{2,1,0:T(8,128)} %e_hbm.1, f32[32,3584]{1,0:T(8,128)} %bitcast.2), custom_call_target="tpu_custom_call" | custom-call | tf_op jit(solution)/shard_map/reduce/pallas_call | solution.py:391
  41.7 2.8 %finish.1 = (bf16[256,3584]{1,0:T(8,128)(2,1)}, f32[1,256,3584]{2,1,0:T(8,128)}, f32[32,3584]{1,0:T(8,128)}) custom-call(f32[4,256,896]{2,1,0:T(8,128)S(1)} %get-tuple-element.9.merged_ref, f32[32,4,896]{2,1,0:T(4,128)S(1)} %get-tuple-element.10.q_ref, bf16[288,192]{1,0:T(8,128)(2,1)S(1)} %get-tuple-element.11.left_ref), custom_call_target="tpu_custom_call" | custom-call | tf_op jit(solution)/shard_map/finish/pallas_call | solution.py:439

commit v7 on v6

--- a/solution.py
+++ b/solution.py
@@ -112,7 +112,7 @@
     for i in range(NX):
         for copy in loads(i):
             copy.start()
-        if i == 1:
+        if i == NX - 1:
             barrier = pltpu.get_barrier_semaphore()
 
             @pl.when(core == 1)
@@ -290,12 +290,12 @@
 
     @pl.when(core == 0)
     def _():
+        for f, r in enumerate(far):
+            to = lax.rem(z + r, NZ) * NX + x
+            send(ag.at[own], aux.at[3 + f], ag_send, aux_recv.at[3 + f], to, mp + 1)
         for j in (2, 1, 3):
             to = z * NX + lax.rem(x + j, NX)
             send(ag.at[own], aux.at[j - 1], ag_send, aux_recv.at[j - 1], to, mp + 1)
-        for f, r in enumerate(far):
-            to = lax.rem(z + r, NZ) * NX + x
-            send(ag.at[own], aux.at[3 + f], ag_send, aux_recv.at[3 + f], to, mp + 1)
         for j in (0, 2, 1, 3):
             spread(ag.at[own], own, 4, j, 0, ag_recv)
         for r in near:
@@ -323,16 +323,16 @@
             wait_bytes(ag.at[piece], agx_recv.at[j])
             for r in near:
                 spread(ag.at[piece], piece, r, 0, 1, ag_recv)
+        for j in (1, 3, 2):
+            piece = lax.rem(x + NX - j, NX) * NZ + z
+            wait_bytes(aux.at[j - 1], aux_recv.at[j - 1])
+            for r in near + (0,):
+                spread(aux.at[j - 1], piece, r, 0, 0, ag_recv)
         for f, r in enumerate(far):
             piece = x * NZ + lax.rem(z + NZ - r, NZ)
             wait_bytes(ag.at[piece], agf_recv.at[f])
             for j in (2, 1, 3):
                 spread(ag.at[piece], piece, 0, j, 1, ag_recv)
-        for j in (1, 3, 2):
-            piece = lax.rem(x + NX - j, NX) * NZ + z
-            wait_bytes(aux.at[j - 1], aux_recv.at[j - 1])
-            for r in near + (0,):
-                spread(aux.at[j - 1], piece, r, 0, 0, ag_recv)
         for f, r in enumerate(far):
             piece = x * NZ + lax.rem(z + NZ - r, NZ)
             wait_bytes(aux.at[3 + f], aux_recv.at[3 + f])

time: 45.1 us -> 45.2 us (level)
  no operation moved by 1% of the time
where the time goes in v7:
time: 45.2 us; the launch traced here: 44.5 us
  Pallas kernels  43.9 us (97%)
  between operations  0.64 us (1%)
    pallas_call x1, Pallas kernels, body(): pl.pallas_call(reduce_kernel, out_shape=(jax.ShapeDtypeStruct((NX, ROWS,...  41.1 us
    pallas_call x1, Pallas kernels, body(): pl.pallas_call(finish_kernel, out_shape=(jax.ShapeDtypeStruct((ROWS, colu...  2.79 us

profile of v7, /device:TPU:8, one launch (start us, length us, event | category | flops | bytes accessed | tf_op | source)
XLA Modules:
  0.0 44.5 jit_solution(120642657104881316)
XLA Ops:
  0.6 41.1 %reduce.1 = (f32[4,256,896]{2,1,0:T(8,128)S(1)}, f32[32,4,896]{2,1,0:T(4,128)S(1)}, bf16[288,192]{1,0:T(8,128)(2,1)S(1)}) custom-call(bf16[1,256,3584]{2,1,0:T(8,128)(2,1)} %g_hbm.1, f32[1,256,3584]{2,1,0:T(8,128)} %e_hbm.1, f32[32,3584]{1,0:T(8,128)} %bitcast.2), custom_call_target="tpu_custom_call" | custom-call | tf_op jit(solution)/shard_map/reduce/pallas_call | solution.py:391
  41.8 2.8 %finish.1 = (bf16[256,3584]{1,0:T(8,128)(2,1)}, f32[1,256,3584]{2,1,0:T(8,128)}, f32[32,3584]{1,0:T(8,128)}) custom-call(f32[4,256,896]{2,1,0:T(8,128)S(1)} %get-tuple-element.9.merged_ref, f32[32,4,896]{2,1,0:T(4,128)S(1)} %get-tuple-element.10.q_ref, bf16[288,192]{1,0:T(8,128)(2,1)S(1)} %get-tuple-element.11.left_ref), custom_call_target="tpu_custom_call" | custom-call | tf_op jit(solution)/shard_map/finish/pallas_call | solution.py:439
